TPU v7x, 32 devices: a whole 2x2x4 slice. The times are simulated.
32 devices in a mesh: groups: 2 (over y), ckpt: 4 (over z), hid: 4 (over x, core).
Axes of the slice: x: 2, y: 2, z: 4, core: 2. Of those that a mesh axis runs over, the one named last changes fastest.
Arguments:
- residual_stream: bfloat16 [4, 768, 2048], P('ckpt', ('groups', 'hid')), parts along dimension 1, may hold values from -6 to 6
- norm_gain: float32 [4, 2048], P('ckpt'), may hold values from 0.1 to 1.9
- norm_shift: float32 [4, 2048], P('ckpt'), may hold values from -3 to 3
- input_weight: bfloat16 [4, 2048, 4096], P('ckpt', None, 'hid'), may hold values from -0.125 to 0.125
- input_bias: float32 [4, 4096], P('ckpt', 'hid'), may hold values from -3 to 3
- output_weight: bfloat16 [4, 4096, 2048], P('ckpt', 'hid'), may hold values from -0.09375 to 0.09375
- output_bias: float32 [4, 2048], P('ckpt'), may hold values from -3 to 3
- encoder_weight: bfloat16 [4, 2048, 4096], P('ckpt', None, 'hid'), may hold values from -0.0625 to 0.0625
- encoder_bias: float32 [4096], P('hid'), may hold values from -3 to 3
- decoder_weight: bfloat16 [4, 4096, 2048], P('ckpt', None, 'hid'), may hold values from -0.09375 to 0.09375
- decoder_bias: float32 [4, 2048], P('ckpt', 'hid'), may hold values from -3 to 3
Outputs:
- latent_codes: bfloat16 [768, 4096], P('groups', 'hid'), parts along dimension 0
- recon_error: float32 [4, 768, 2048], P('ckpt', 'groups', 'hid'), parts along dimension 1
There are 2 independent parts, one for each index of `groups`. A program takes and returns all parts, laid end to end along the dimension named above; an argument that names none is the same for every part. Nothing has to cross between parts.
All inputs are finite; a program needn't handle non-finite values.
Results may differ from a plain program's by a relative error of at most 0.0056.
Values may be sent and summed in bfloat16 or wider, within the bound.
A program may use at most 64 MiB of HBM per device.

v0:
```python
import jax
import jax.numpy as jnp
from jax import lax
from jax.sharding import PartitionSpec as P


def per_device(
    residual_stream,
    norm_gain,
    norm_shift,
    input_weight,
    input_bias,
    output_weight,
    output_bias,
    encoder_weight,
    encoder_bias,
    decoder_weight,
    decoder_bias,
):
    values = residual_stream[0].astype(jnp.float32)
    average = jnp.mean(values, axis=-1, keepdims=True)
    centred = values - average
    variance = jnp.mean(centred * centred, axis=-1, keepdims=True)
    normed = (centred * lax.rsqrt(variance + 1e-05) * norm_gain[0] + norm_shift[0]).astype(
        jnp.bfloat16
    )
    first_weight = input_weight[0]
    first_bias = input_bias[0]
    second_weight = output_weight[0]
    hidden = jax.nn.gelu(
        jnp.dot(
            lax.all_gather(normed, "hid", axis=0, tiled=True),
            first_weight,
            preferred_element_type=jnp.float32,
        )
        + first_bias,
        approximate=False,
    ).astype(jnp.bfloat16)
    partial_out = jnp.dot(hidden, second_weight, preferred_element_type=jnp.float32)
    mlp_out = (lax.psum(partial_out, "hid") + output_bias[0]).astype(jnp.bfloat16)
    encoder_terms = jnp.dot(mlp_out, encoder_weight[0], preferred_element_type=jnp.float32)
    latent_codes = jax.nn.relu(lax.psum(encoder_terms, "ckpt") + encoder_bias).astype(jnp.bfloat16)
    local_decoder = decoder_weight[0]
    column_count = local_decoder.shape[1]
    rebuilt = (
        jnp.dot(
            lax.all_gather(latent_codes, "hid", axis=1, tiled=True),
            local_decoder,
            preferred_element_type=jnp.float32,
        )
        + decoder_bias[0]
    )
    own_columns = lax.dynamic_slice_in_dim(
        mlp_out, lax.axis_index("hid") * column_count, column_count, 1
    ).astype(jnp.float32)
    recon_error = (own_columns - rebuilt)[None]
    return (latent_codes, recon_error)


def solution(mesh):
    placed = (
        P("ckpt", ("groups", "hid"), None),
        P("ckpt", None),
        P("ckpt", None),
        P("ckpt", None, "hid"),
        P("ckpt", "hid"),
        P("ckpt", "hid", None),
        P("ckpt", None),
        P("ckpt", None, "hid"),
        P("hid"),
        P("ckpt", None, "hid"),
        P("ckpt", "hid"),
    )
    return jax.shard_map(
        per_device,
        mesh=mesh,
        in_specs=placed,
        out_specs=(P("groups", "hid"), P("ckpt", "groups", "hid")),
        check_vma=False,
    )
```

profile of v0, /device:TPU:0, one launch (start us, length us, event | category | flops | bytes accessed | tf_op | source)
XLA Modules:
  0.0 233.3 jit_solution(14858888776073998837)
XLA Ops:
  7.2 0.0 copy-start.3
  7.2 0.0 all-gather.3.cloned.1.call-start
  7.2 1.1 convert_reduce_fusion
  8.4 1.3 fusion.34
  9.7 2.1 fusion.37
  11.7 0.0 all-gather.3.cloned.1.call-update
  11.8 0.0 all-reduce.3.cloned.1.call-start
  11.8 22.5 %all-gather.3.cloned.1.call-done = bf16[384,2048]{1,0:T(8,128)(2,1)} async-done(((bf16[96,2048]{1,0:T(8,128)(2,1)}), bf16[384,2048]{1,0:T(8,128)(2,1)}) %all-gather.3.cloned.1.call-update) | async-done | bytes 1572880 | tf_op jit(solution)/shard_map/all_gather | solution.py:32
  34.3 12.3 %fusion.4 = f32[384,2048]{1,0:T(8,128)} fusion(bf16[1,1024,2048]{2,1,0:T(8,128)(2,1)} %param.16, bf16[384,2048]{1,0:T(8,128)(2,1)} %all-gather.3.cloned.1.call-done, bf16[1,2048,1024]{2,1,0:T(8,128)(2,1)} %param.14, f32[1024]{0:T(1024)S(1)} %bitcast.51), kind=kOutput, calls=%fused_computation.4 | convolution fusion | flops 3247177728 | bytes 13111296 | tf_op jit(solution)/shard_map/dot_general | solution.py:39
  46.5 0.0 all-reduce.3.cloned.1.call-update
  46.6 0.0 all-reduce.5.cloned.1.call-start
  46.6 68.5 %all-reduce.3.cloned.1.call-done = f32[384,2048]{1,0:T(8,128)} async-done(((f32[384,2048]{1,0:T(8,128)}), f32[384,2048]{1,0:T(8,128)}) %all-reduce.3.cloned.1.call-update) | async-done | bytes 3145744 | tf_op jit(solution)/shard_map/psum | solution.py:40
  115.1 2.4 %add_convert_fusion = bf16[384,2048]{1,0:T(8,128)(2,1)S(1)} fusion(f32[384,2048]{1,0:T(8,128)} %all-reduce.3.cloned.1.call-done, f32[2048]{0:T(1024)S(1)} %bitcast.50), kind=kLoop, calls=%fused_computation.8 | loop fusion | flops 1572864 | bytes 4726784 | tf_op jit(solution)/shard_map/convert_element_type | solution.py:40
  117.5 0.8 copy-done.2
  118.3 3.0 %fusion.2 = f32[384,1024]{1,0:T(8,128)} fusion(bf16[384,2048]{1,0:T(8,128)(2,1)S(1)} %add_convert_fusion, bf16[1,2048,1024]{2,1,0:T(8,128)(2,1)S(1)} %copy-done.2), kind=kOutput, calls=%fused_computation.2 | convolution fusion | flops 1610612736 | bytes 7340032 | tf_op jit(solution)/shard_map/dot_general | solution.py:41
  121.3 0.0 all-reduce.5.cloned.1.call-update
  121.3 0.0 copy-start.4
  121.3 0.0 all-gather.5.cloned.1.call-start
  121.3 69.3 %all-reduce.5.cloned.1.call-done = f32[384,1024]{1,0:T(8,128)} async-done(((f32[384,1024]{1,0:T(8,128)}), f32[384,1024]{1,0:T(8,128)}) %all-reduce.5.cloned.1.call-update) | async-done | bytes 1572880 | tf_op jit(solution)/shard_map/psum | solution.py:42
  190.7 2.5 %maximum_convert_fusion = bf16[384,1024]{1,0:T(8,128)(2,1)} fusion(f32[384,1024]{1,0:T(8,128)} %all-reduce.5.cloned.1.call-done, f32[1024]{0:T(1024)S(1)} %copy-done.1), kind=kLoop, calls=%fused_computation.13 | loop fusion | flops 1179648 | bytes 2363392 | tf_op jit(solution)/shard_map/convert_element_type | solution.py:42
  193.1 0.0 all-gather.5.cloned.1.call-update
  193.2 27.7 %all-gather.5.cloned.1.call-done = bf16[384,4096]{1,0:T(8,128)(2,1)} async-done(((bf16[384,1024]{1,0:T(8,128)(2,1)}), bf16[384,4096]{1,0:T(8,128)(2,1)}) %all-gather.5.cloned.1.call-update) | async-done | bytes 3145744 | tf_op jit(solution)/shard_map/all_gather | solution.py:47
  220.9 0.0 copy-done.4
  220.9 5.8 %fusion.26 = f32[1,384,512]{2,1,0:T(8,128)} fusion(bf16[384,4096]{1,0:T(8,128)(2,1)} %all-gather.5.cloned.1.call-done, bf16[1,4096,512]{2,1,0:T(8,128)(2,1)} %param.20, f32[512]{0:T(512)S(1)} %bitcast.52, bf16[384,2048]{1,0:T(8,128)(2,1)S(1)} %add_convert_fusion, s32[]{:T(128)S(6)} %select_n.3), kind=kOutput, calls=%fused_computation.31 | convolution fusion | flops 1611202560 | bytes 8521732 | tf_op jit(solution)/shard_map/dot_general | solution.py:46
  (8 shorter events, 0.0 us)
Async XLA Ops:
  7.2 27.1 %copy-start.3 = (f32[1,1024]{1,0:T(1,128)S(1)}, f32[1,1024]{1,0:T(1,128)}, u32[]{:S(2)}) copy-start(f32[1,1024]{1,0:T(1,128)} %param.15) | copy-start | bytes 12292
  7.2 27.1 %all-gather.3.cloned.1.call-start = ((), (), s32[]{:S(2)}) async-start(), calls=%async_computation | async-start | bytes 1966080 | tf_op jit(solution)/shard_map/all_gather | solution.py:32
  11.8 103.4 %all-reduce.3.cloned.1.call-start = ((), (), s32[]{:S(2)}) async-start(), calls=%async_computation.1 | async-start | bytes 6291456 | tf_op jit(solution)/shard_map/psum | solution.py:40
  46.5 68.6 %copy-start = (f32[1,2048]{1,0:T(1,128)S(1)}, f32[1,2048]{1,0:T(1,128)}, u32[]{:S(2)}) copy-start(f32[1,2048]{1,0:T(1,128)} %param.17) | copy-start | bytes 24580
  46.6 144.1 %all-reduce.5.cloned.1.call-start = ((), (), s32[]{:S(2)}) async-start(), calls=%async_computation.2 | async-start | bytes 3145728 | tf_op jit(solution)/shard_map/psum | solution.py:42
  115.1 3.1 %copy-start.2 = (bf16[1,2048,1024]{2,1,0:T(8,128)(2,1)S(1)}, bf16[1,2048,1024]{2,1,0:T(8,128)(2,1)}, u32[]{:S(2)}) copy-start(bf16[1,2048,1024]{2,1,0:T(8,128)(2,1)} %param.18) | copy-start | bytes 12582916
  121.3 69.4 %copy-start.1 = (f32[1024]{0:T(1024)S(1)}, f32[1024]{0:T(1024)}, u32[]{:S(2)}) copy-start(f32[1024]{0:T(1024)} %param.19) | copy-start | bytes 12292
  121.3 99.6 %copy-start.4 = (f32[1,512]{1,0:T(1,128)S(1)}, f32[1,512]{1,0:T(1,128)}, u32[]{:S(2)}) copy-start(f32[1,512]{1,0:T(1,128)} %param.21) | copy-start | bytes 6148
  121.3 99.6 %all-gather.5.cloned.1.call-start = ((), (), s32[]{:S(2)}) async-start(), calls=%async_computation.3 | async-start | bytes 3932160 | tf_op jit(solution)/shard_map/all_gather | solution.py:47
Sparse Core Ops, SparseCore 0:
  11.9 22.3 all-gather.2
  46.7 68.4 all-reduce.2
  121.4 69.2 all-reduce.4
  193.3 27.5 all-gather.4
where the time goes:
time: 233 us
  waiting for transfers between devices  188 us (81%)
  matrix products  21 us (9%)
  between operations  13.8 us (6%)
  other arithmetic  9.33 us (4%)
    psum x1, waiting for transfers between devices, per_device(): lax.psum(encoder_terms, 'ckpt') + encoder_bias  69.3 us
    psum x1, waiting for transfers between devices, per_device(): lax.psum(partial_out, 'hid') + output_bias[0]  68.5 us
    all_gather x1, waiting for transfers between devices, per_device(): lax.all_gather(latent_codes, 'hid', axis=1, tiled=True)  27.7 us
    all_gather x1, waiting for transfers between devices, per_device(): lax.all_gather(normed, 'hid', axis=0, tiled=True)  22.5 us
    dot_general x1, matrix products, per_device(): jnp.dot(hidden, second_weight, preferred_element_type=jnp.float32)  12.3 us
    dot_general x1, matrix products, per_device(): jnp.dot(lax.all_gather(latent_codes, 'hid', axis=1, tiled=True), local_de...  5.81 us
  transfers between devices with their start and end apart: 4, of which 4 were waited for; matrix products, arithmetic and copies ran while one was open for 0% of the time, Pallas kernels for 0%

commit v1 on v0

--- a/solution.py
+++ b/solution.py
@@ -2,6 +2,18 @@
 import jax.numpy as jnp
 from jax import lax
 from jax.sharding import PartitionSpec as P
+
+
+def gather_by_bits(array, axis, dim):
+    ways, here = (lax.axis_size(axis), lax.axis_index(axis))
+    grown, reach = (array, 1)
+    while reach < ways:
+        theirs = lax.ppermute(grown, axis, [(d, d ^ reach) for d in range(ways)])
+        mine_first = jnp.concatenate([grown, theirs], axis=dim)
+        theirs_first = jnp.concatenate([theirs, grown], axis=dim)
+        grown = jnp.where(here & reach == 0, mine_first, theirs_first)
+        reach = 2 * reach
+    return grown
 
 
 def per_device(
@@ -44,7 +56,7 @@
     column_count = local_decoder.shape[1]
     rebuilt = (
         jnp.dot(
-            lax.all_gather(latent_codes, "hid", axis=1, tiled=True),
+            gather_by_bits(latent_codes, "hid", 1),
             local_decoder,
             preferred_element_type=jnp.float32,
         )

time: 233 us -> 247 us (1.060)
  waiting for transfers between devices: 188 us -> 198 us
    ppermute x0 -> x2, waiting for transfers between devices: none -> 37.5 us  [gather_by_bits(): theirs = lax.ppermute(grown, axis, [(d, d ^ reach) for d in range(ways)])]
    all_gather x1 -> x0, waiting for transfers between devices: 27.7 us -> none  [per_device(): lax.all_gather(latent_codes, 'hid', axis=1, tiled=True)]
  transfers between devices with their start and end apart: 4 -> 5, of which waited for: 4 -> 5; matrix products, arithmetic and copies ran while one was open for 0% -> 0% of each run, Pallas kernels for 0% -> 0%
where the time goes in v1:
time: 247 us
  waiting for transfers between devices  198 us (80%)
  matrix products  22.2 us (9%)
  between operations  13.8 us (6%)
  other arithmetic  10.2 us (4%)
    psum x1, waiting for transfers between devices, per_device(): lax.psum(encoder_terms, 'ckpt') + encoder_bias  69.4 us
    psum x1, waiting for transfers between devices, per_device(): lax.psum(partial_out, 'hid') + output_bias[0]  68.6 us
    ppermute x2, waiting for transfers between devices, gather_by_bits(): theirs = lax.ppermute(grown, axis, [(d, d ^ reach) for d in range(ways)])  37.5 us
    all_gather x1, waiting for transfers between devices, per_device(): lax.all_gather(normed, 'hid', axis=0, tiled=True)  22.5 us
    dot_general x1, matrix products, per_device(): jnp.dot(hidden, second_weight, preferred_element_type=jnp.float32)  12.3 us
    dot_general x1, matrix products, per_device(): jnp.dot(gather_by_bits(latent_codes, 'hid', 1), local_decoder, preferred_...  6.95 us
  transfers between devices with their start and end apart: 5, of which 5 were waited for; matrix products, arithmetic and copies ran while one was open for 0% of the time, Pallas kernels for 0%

profile of v1, /device:TPU:0, one launch (start us, length us, event | category | flops | bytes accessed | tf_op | source)
XLA Modules:
  0.0 246.6 jit_solution(1896454708840933690)
XLA Ops:
  7.2 0.0 all-gather.2.cloned.1.call-start
  7.2 1.1 convert_reduce_fusion
  8.4 1.3 fusion.40
  9.7 2.1 fusion.43
  11.7 0.0 all-gather.2.cloned.1.call-update
  11.8 0.0 all-reduce.3.cloned.1.call-start
  11.8 22.5 %all-gather.2.cloned.1.call-done = bf16[384,2048]{1,0:T(8,128)(2,1)} async-done(((bf16[96,2048]{1,0:T(8,128)(2,1)}), bf16[384,2048]{1,0:T(8,128)(2,1)}) %all-gather.2.cloned.1.call-update) | async-done | bytes 1572880 | tf_op jit(solution)/shard_map/all_gather | solution.py:44
  34.3 12.3 %fusion.4 = f32[384,2048]{1,0:T(8,128)} fusion(bf16[1,1024,2048]{2,1,0:T(8,128)(2,1)} %param.16, bf16[384,2048]{1,0:T(8,128)(2,1)} %all-gather.2.cloned.1.call-done, bf16[1,2048,1024]{2,1,0:T(8,128)(2,1)} %param.14, f32[1024]{0:T(1024)S(1)} %bitcast.50), kind=kOutput, calls=%fused_computation.4 | convolution fusion | flops 3247177728 | bytes 13111296 | tf_op jit(solution)/shard_map/dot_general | solution.py:51
  46.5 0.0 all-reduce.3.cloned.1.call-update
  46.6 0.0 all-reduce.5.cloned.1.call-start
  46.6 68.6 %all-reduce.3.cloned.1.call-done = f32[384,2048]{1,0:T(8,128)} async-done(((f32[384,2048]{1,0:T(8,128)}), f32[384,2048]{1,0:T(8,128)}) %all-reduce.3.cloned.1.call-update) | async-done | bytes 3145744 | tf_op jit(solution)/shard_map/psum | solution.py:52
  115.2 2.4 add_convert_fusion
  117.5 0.8 copy-done.3
  118.3 3.0 %fusion.2 = f32[384,1024]{1,0:T(8,128)} fusion(bf16[384,2048]{1,0:T(8,128)(2,1)S(1)} %add_convert_fusion, bf16[1,2048,1024]{2,1,0:T(8,128)(2,1)S(1)} %copy-done.3), kind=kOutput, calls=%fused_computation.2 | convolution fusion | flops 1610612736 | bytes 7340032 | tf_op jit(solution)/shard_map/dot_general | solution.py:53
  121.3 0.0 all-reduce.5.cloned.1.call-update
  121.3 69.4 %all-reduce.5.cloned.1.call-done = f32[384,1024]{1,0:T(8,128)} async-done(((f32[384,1024]{1,0:T(8,128)}), f32[384,1024]{1,0:T(8,128)}) %all-reduce.5.cloned.1.call-update) | async-done | bytes 1572880 | tf_op jit(solution)/shard_map/psum | solution.py:54
  190.7 1.6 maximum_convert_fusion
  192.3 0.0 copy-start
  192.3 0.1 collective-permute-start
  192.4 2.3 collective-permute-done
  194.6 1.8 maximum_select_fusion.2
  196.4 1.5 collective-permute-start.1
  197.9 35.3 %collective-permute-done.1 = bf16[384,2048]{1,0:T(8,128)(2,1)} collective-permute-done((bf16[384,2048]{1,0:T(8,128)(2,1)}, bf16[384,2048]{1,0:T(8,128)(2,1)}, u32[]{:S(2)}, u32[]{:S(2)}) %collective-permute-start.1) | collective-permute-done | bytes 1572896 | tf_op jit(solution)/shard_map/ppermute | solution.py:11
  233.1 6.9 %fusion.32 = f32[1,384,512]{2,1,0:T(8,128)} fusion(bf16[1,4096,512]{2,1,0:T(8,128)(2,1)} %param.20, bf16[384,2048]{1,0:T(8,128)(2,1)} %collective-permute-done.1, bf16[384,2048]{1,0:T(8,128)(2,1)} %maximum_select_fusion.2, pred[]{:T(512)S(6)} %eq.6, f32[512]{0:T(512)S(1)} %bitcast.51, bf16[384,2048]{1,0:T(8,128)(2,1)S(1)} %add_convert_fusion, s32[]{:T(128)S(6)} %select_n.19), kind=kOutput, calls=%fused_computation.39 | convolution fusion | flops 1625358336 | bytes 8521733 | tf_op jit(solution)/shard_map/dot_general | solution.py:58
  (12 shorter events, 0.0 us)
Async XLA Ops:
  7.2 27.1 %copy-start.4 = (f32[1,1024]{1,0:T(1,128)S(1)}, f32[1,1024]{1,0:T(1,128)}, u32[]{:S(2)}) copy-start(f32[1,1024]{1,0:T(1,128)} %param.15) | copy-start | bytes 12292
  7.2 27.1 %all-gather.2.cloned.1.call-start = ((), (), s32[]{:S(2)}) async-start(), calls=%async_computation | async-start | bytes 1966080 | tf_op jit(solution)/shard_map/all_gather | solution.py:44
  11.8 103.4 %all-reduce.3.cloned.1.call-start = ((), (), s32[]{:S(2)}) async-start(), calls=%async_computation.1 | async-start | bytes 6291456 | tf_op jit(solution)/shard_map/psum | solution.py:52
  46.5 68.6 %copy-start.1 = (f32[1,2048]{1,0:T(1,128)S(1)}, f32[1,2048]{1,0:T(1,128)}, u32[]{:S(2)}) copy-start(f32[1,2048]{1,0:T(1,128)} %param.17) | copy-start | bytes 24580
  46.6 144.1 %all-reduce.5.cloned.1.call-start = ((), (), s32[]{:S(2)}) async-start(), calls=%async_computation.2 | async-start | bytes 3145728 | tf_op jit(solution)/shard_map/psum | solution.py:54
  115.2 3.1 %copy-start.3 = (bf16[1,2048,1024]{2,1,0:T(8,128)(2,1)S(1)}, bf16[1,2048,1024]{2,1,0:T(8,128)(2,1)}, u32[]{:S(2)}) copy-start(bf16[1,2048,1024]{2,1,0:T(8,128)(2,1)} %param.18) | copy-start | bytes 12582916
  121.3 69.4 %copy-start.2 = (f32[1024]{0:T(1024)S(1)}, f32[1024]{0:T(1024)}, u32[]{:S(2)}) copy-start(f32[1024]{0:T(1024)} %param.19) | copy-start | bytes 12292
  192.3 4.1 %copy-start = (bf16[384,1024]{1,0:T(8,128)(2,1)}, bf16[384,1024]{1,0:T(8,128)(2,1)S(1)}, u32[]{:S(2)}) copy-start(bf16[384,1024]{1,0:T(8,128)(2,1)S(1)} %maximum_convert_fusion) | copy-start | bytes 2359300
  192.3 2.4 collective-permute-start
  192.4 40.8 %copy-start.5 = (f32[1,512]{1,0:T(1,128)S(1)}, f32[1,512]{1,0:T(1,128)}, u32[]{:S(2)}) copy-start(f32[1,512]{1,0:T(1,128)} %param.21) | copy-start | bytes 6148
  196.4 36.8 %collective-permute-start.1 = (bf16[384,2048]{1,0:T(8,128)(2,1)}, bf16[384,2048]{1,0:T(8,128)(2,1)}, u32[]{:S(2)}, u32[]{:S(2)}) collective-permute-start(bf16[384,2048]{1,0:T(8,128)(2,1)} %maximum_select_fusion.2), channel_id=1, source_target_pairs={{0,2},{1,3},{2,0},{3,1},{4,6},{5,7},{6,4},{7,5},{8,10},{9,11},{10,... | collective-permute-start | bytes 4718600 | tf_op jit(solution)/shard_map/ppermute | solution.py:11
Sparse Core Ops, SparseCore 0:
  11.9 22.3 all-gather.1
  46.7 68.4 all-reduce.2
  121.4 69.2 all-reduce.4
